TPU v7x, 512 devices: a whole 4x4x16 slice. The times are simulated.
512 devices in a mesh: slab: 8 (over y, core), sub: 64 (over z, x).
Axes of the slice: x: 4, y: 4, z: 16, core: 2. Of those that a mesh axis runs over, the one named last changes fastest.
Arguments:
- source: float32 [4096, 343], P(('slab', 'sub')), may hold values from -8 to 8
- conductivity: float32 [4096], P(('slab', 'sub')), may hold values from 0.1 to 10
- basis: float32 [64, 4096, 343], P(None, ('slab', 'sub'))
- current_values: bfloat16 [131072, 343], P(('slab', 'sub')), may hold values from -6 to 6
- current_elements: int32 [131072], P(('slab', 'sub')), may hold values from 0 to 7
- current_owners: int32 [131072, 1], P(('slab', 'sub')), may hold values from 0 to 63; in each aligned block of 256 rows (0 to 255, 256 to 511, ...) at most 6 rows name the same one
- block_counts: int32 [512], P(('slab', 'sub')), may hold values from 1 to 2, as said below
Outputs:
- solution: float32 [4096, 343], P(('slab', 'sub'))
- residual: float32 [4096, 343], P(('slab', 'sub'))
Inputs may be any that keep to these rules, and one draw needn't show every extreme that they name: `current_owners`: within the rows of one device at most 6 rows name any one owner, and some device's rows name one owner exactly 6 times. `block_counts`: rows in blocks at or beyond a device's count are padding and carry nothing; some device holds 2 blocks.
All inputs are finite; a program needn't handle non-finite values.
Results may differ from a plain program's by a relative error of at most 0.0006.
Values may be sent and summed in bfloat16 or wider, within the bound.
A program may use at most 128 MiB of HBM per device.

v0:
```python
import jax
import jax.numpy as jnp
from jax import lax
from jax.sharding import PartitionSpec as P

BLOCK = 128
ITERS = 3


penalty = 10.0
relaxation = 0.2
highest = lax.Precision.HIGHEST


def extended_2(value, sides, width):
    for axis, dim in sides:
        size, length = (lax.axis_size(axis), value.shape[dim])
        up = [(i, (i + 1) % size) for i in range(size - 1)]
        down = [(j, i) for i, j in up]
        last = lax.slice_in_dim(value, length - width, length, axis=dim)
        first = lax.slice_in_dim(value, 0, width, axis=dim)
        before = lax.ppermute(last, axis, up)
        after = lax.ppermute(first, axis, down)
        value = jnp.concatenate([before, value, after], axis=dim)
    return value


def element_matrix():
    points = jnp.arange(7)
    at_ends = ((points == 0) | (points == 6)).astype(jnp.float32)
    second = jnp.diag(2.0 - at_ends) - (jnp.abs(points[:, None] - points[None, :]) == 1).astype(
        jnp.float32
    )
    identity = jnp.eye(7, dtype=jnp.float32)
    return (
        jnp.kron(jnp.kron(second, identity), identity)
        + jnp.kron(jnp.kron(identity, second), identity)
        + jnp.kron(identity, jnp.kron(identity, second))
    )


def face_mask():
    node_ids = jnp.arange(343)
    return ((node_ids < 49) | (node_ids >= 294)).astype(jnp.float32)


def couple(field, conductivity, stiffness, prev_right, next_left):
    left_term = penalty * (field[..., :49] - prev_right)
    right_term = penalty * (field[..., 294:] - next_left)
    middle = jnp.zeros(field.shape[:-1] + (245,), jnp.float32)
    return (
        conductivity[:, None] * stiffness
        + relaxation * field
        + jnp.concatenate([left_term, middle, right_term], axis=-1)
    )


def local_faces(field):
    return jnp.concatenate([field[..., :49], field[..., 294:]], axis=-1)


def rims(faces):
    return extended_2(faces, ((("slab", "sub"), 1),), 1)


def apply_field(field, conductivity, kel):
    stiffness = jnp.dot(field, kel, precision=highest, preferred_element_type=jnp.float32)
    extended = rims(local_faces(field)[None])[0]
    return couple(field, conductivity, stiffness, extended[:-2, 49:], extended[2:, :49])


def apply_block(sub_basis, conductivity, kel):
    stiffness = jnp.dot(
        sub_basis.reshape(-1, 343), kel, precision=highest, preferred_element_type=jnp.float32
    ).reshape(sub_basis.shape)
    prev_right = jnp.pad(sub_basis[:, :-1, 294:], ((0, 0), (1, 0), (0, 0)))
    next_left = jnp.pad(sub_basis[:, 1:, :49], ((0, 0), (0, 1), (0, 0)))
    return couple(sub_basis, conductivity, stiffness, prev_right, next_left)


def invert(matrix):
    factor = jnp.linalg.cholesky(matrix)
    identity = jnp.eye(matrix.shape[0], dtype=jnp.float32)
    solved = lax.linalg.triangular_solve(factor, identity, left_side=True, lower=True)
    return jnp.dot(solved.T, solved, precision=highest, preferred_element_type=jnp.float32)


def matvec(matrix, vector):
    return jnp.dot(matrix, vector, precision=highest, preferred_element_type=jnp.float32)


def on_device(
    source, conductivity, basis, current_values, current_elements, current_owners, block_counts
):
    kel = element_matrix()
    diagonal = (
        conductivity[:, None] * jnp.diagonal(kel)[None, :]
        + relaxation
        + penalty * face_mask()[None, :]
    )
    row_count = current_values.shape[0]
    elements = source.shape[0]
    is_live = jnp.arange(row_count) // BLOCK < block_counts[0]
    owners = current_owners[:, 0]
    element_ids = (jnp.arange(elements) + 1).astype(jnp.float32)
    marks = jnp.stack([jnp.where(is_live, owners + 1, 0), current_elements + 1], axis=1).astype(
        jnp.bfloat16
    )
    own_index = (lax.axis_index("sub") + 1).astype(jnp.float32)
    row_values = lax.all_gather(current_values, "sub", axis=0, tiled=True)
    row_marks = lax.all_gather(marks, "sub", axis=0, tiled=True)
    wide_marks = row_marks.astype(jnp.float32)
    select = (wide_marks[None, :, 0] == own_index) & (
        wide_marks[None, :, 1] == element_ids[:, None]
    )
    currents = jnp.dot(select.astype(jnp.bfloat16), row_values, preferred_element_type=jnp.float32)
    rhs = source + currents
    applied_basis = apply_block(basis, conductivity, kel)
    matrix = jnp.einsum("kep,lep->kl", basis, applied_basis, precision=highest)
    inverse = invert(matrix)
    extended = rims(local_faces(basis))
    left_block = -penalty * jnp.dot(
        basis[:, 0, :49],
        extended[:, 0, 49:].T,
        precision=highest,
        preferred_element_type=jnp.float32,
    )
    right_block = -penalty * jnp.dot(
        basis[:, -1, 294:],
        extended[:, -1, :49].T,
        precision=highest,
        preferred_element_type=jnp.float32,
    )

    def precondition(residual):
        projected = jnp.einsum("kep,ep->k", basis, residual, precision=highest)
        first_pass = matvec(inverse, projected)
        beside_all = extended_2(first_pass[None, :], ((("slab", "sub"), 0),), 1)
        corrected = (
            projected - matvec(left_block, beside_all[0]) - matvec(right_block, beside_all[2])
        )
        second_pass = matvec(inverse, corrected)
        return residual / diagonal + jnp.einsum("kep,k->ep", basis, second_pass, precision=highest)

    def residual_inner(residual, precond):
        return lax.psum(jnp.sum(residual * precond), ("slab", "sub"))

    solution = jnp.zeros_like(rhs)
    residual = rhs
    precond = precondition(residual)
    direction = precond
    inner_now = residual_inner(residual, precond)
    for iteration in range(ITERS):
        applied = apply_field(direction, conductivity, kel)
        step_size = inner_now / lax.psum(jnp.sum(direction * applied), ("slab", "sub"))
        solution = solution + step_size * direction
        residual = residual - step_size * applied
        if iteration + 1 < ITERS:
            precond = precondition(residual)
            inner_next = residual_inner(residual, precond)
            direction = precond + inner_next / inner_now * direction
            inner_now = inner_next
    return (solution, residual)


def solution(mesh):
    placed = (
        P(("slab", "sub"), None),
        P(("slab", "sub")),
        P(None, ("slab", "sub"), None),
        P(("slab", "sub"), None),
        P(("slab", "sub")),
        P(("slab", "sub"), None),
        P(("slab", "sub")),
    )
    return jax.shard_map(
        on_device,
        mesh=mesh,
        in_specs=placed,
        out_specs=(P(("slab", "sub"), None), P(("slab", "sub"), None)),
        check_vma=False,
    )
```

profile of v0, /device:TPU:1, one launch (start us, length us, event | category | flops | bytes accessed | tf_op | source)
XLA Modules:
  0.0 806.1 jit_solution(544420401441714989)
XLA Ops:
  7.2 0.7 all-gather.2.cloned.1.call-update
  7.9 1.2 fusion.71
  9.1 1.2 fusion.70
  10.5 4.0 collective-permute-start
  14.4 12.7 %collective-permute-start.2 = (f32[64,1,98]{2,1,0:T(1,128)S(1)}, f32[64,1,98]{2,1,0:T(1,128)S(1)}, u32[]{:S(2)}, u32[]{:S(2)}) collective-permute-start(f32[64,1,98]{2,1,0:T(1,128)S(1)} %get-tuple-element.16), channel_id=1, source_target_pairs={{1,0},{2,1},{3,2},{4,3},{5,4},{6,5},{7,6},{8,7},{9,8},{10,9},{11,1... | collective-permute-start | bytes 75272 | tf_op jit(solution)/shard_map/ppermute | solution.py:23
  27.1 0.7 add_convert_fusion
  28.5 0.7 fusion.54
  29.2 63.1 %all_gather.6 = bf16[16384,2]{0,1:T(2,128)(2,1)S(1)} all-gather(bf16[256,2]{0,1:T(2,128)(2,1)S(1)} %pad_maximum_fusion.2), channel_id=1, replica_groups=mesh['slab'=8,'sub'=64] {'sub'}, dimensions={0}, use_global_device_ids=true | all-gather | bytes 66560 | tf_op jit(solution)/shard_map/all_gather | solution.py:111
  93.1 7.1 mul.466
  100.2 10.2 %broadcast_multiply_fusion = (f32[49,7,49,7]{3,2,1,0:T(8,128)}, f32[49,7,49,7]{3,2,1,0:T(8,128)}) fusion(f32[49,49]{1,0:T(8,128)S(1)} %get-tuple-element.6, f32[7,7]{1,0:T(8,128)S(1)} %fusion.51, f32[49,7,49,7]{3,2,1,0:T(8,128)} %mul.466, f32[49,49]{1,0:T(8,128)S(1)} %mul.450), kind=kLoop, calls=%fused_computation.2 | loop fusion | flops 352947 | bytes 1431192 | tf_op jit(solution)/shard_map/add | solution.py:36
  110.4 6.3 add.174
  116.7 2.1 convolution_bitcast_fusion
  119.3 0.9 convolution_bitcast_fusion.1
  120.4 5.8 cholesky.17
  127.5 4.9 custom-call.6
  133.5 6.2 add.168
  140.3 5.5 gather_fusion
  145.7 0.9 slice.142
  146.8 45.0 %all-gather.2.cloned.1.call-done = bf16[16384,343]{0,1:T(8,128)(2,1)} async-done(((bf16[256,343]{0,1:T(8,128)(2,1)}), bf16[16384,343]{0,1:T(8,128)(2,1)}) %all-gather.2.cloned.1.call-update) | async-done | bytes 11239440 | tf_op jit(solution)/shard_map/all_gather | solution.py:110
  191.9 7.2 convolution_add_fusion
  199.1 0.7 fusion.32
  200.0 2.3 collective-permute-start.1
  202.5 11.9 %collective-permute-start.3 = (f32[1,64]{1,0:T(1,128)S(1)}, f32[1,64]{1,0:T(1,128)S(1)}, u32[]{:S(2)}, u32[]{:S(2)}) collective-permute-start(f32[1,64]{1,0:T(1,128)S(1)} %fusion.60), channel_id=1, source_target_pairs={{1,0},{2,1},{3,2},{4,3},{5,4},{6,5},{7,6},{8,7},{9,8},{10,9},{11,1... | collective-permute-start | bytes 776 | tf_op jit(solution)/shard_map/ppermute | solution.py:23
  216.2 7.5 collective-permute-start.5
  223.7 1.9 collective-permute-start.4
  225.7 6.2 collective-permute-done.4
  232.0 1.0 multiply_reduce_fusion.4
  233.0 105.4 %all-reduce.2 = (f32[]{:T(128)}, f32[]{:T(128)}) all-reduce(f32[]{:T(128)} %get-tuple-element.3, f32[]{:T(128)} %get-tuple-element.2), channel_id=1, replica_groups=mesh['slab'=8,'sub'=64] {'slab','sub'}, use_global_device_ids=true, to_apply=%region_3.4 | all-reduce | flops 2 | bytes 16 | tf_op jit(solution)/shard_map/psum | solution.py:146
  339.8 0.7 fusion.28
  340.7 1.9 collective-permute-start.6
  342.6 7.0 collective-permute-start.7
  351.2 0.7 multiply_reduce_fusion.3
  351.8 103.4 %psum.44 = f32[]{:T(128)} all-reduce(f32[]{:T(128)} %multiply_reduce_fusion.3), channel_id=1, replica_groups=mesh['slab'=8,'sub'=64] {'slab','sub'}, use_global_device_ids=true, to_apply=%region_7.8 | all-reduce | flops 1 | bytes 8 | tf_op jit(solution)/shard_map/psum | solution.py:146
  456.8 2.7 collective-permute-start.9
  459.6 2.5 collective-permute-start.8
  462.1 5.6 collective-permute-done.8
  467.8 1.0 multiply_reduce_fusion.2
  468.8 98.8 %psum.45 = f32[]{:T(128)} all-reduce(f32[]{:T(128)} %get-tuple-element.39), channel_id=1, replica_groups=mesh['slab'=8,'sub'=64] {'slab','sub'}, use_global_device_ids=true, to_apply=%region_9.10 | all-reduce | flops 1 | bytes 8 | tf_op jit(solution)/shard_map/psum | solution.py:155
  569.0 0.7 fusion.24
  569.9 2.0 collective-permute-start.10
  571.9 6.9 collective-permute-start.11
  580.4 0.7 multiply_reduce_fusion.1
  581.1 103.4 %psum.46 = f32[]{:T(128)} all-reduce(f32[]{:T(128)} %multiply_reduce_fusion.1), channel_id=1, replica_groups=mesh['slab'=8,'sub'=64] {'slab','sub'}, use_global_device_ids=true, to_apply=%region_11.12 | all-reduce | flops 1 | bytes 8 | tf_op jit(solution)/shard_map/psum | solution.py:146
  686.0 3.7 collective-permute-start.13
  689.7 1.9 collective-permute-start.12
  691.6 6.2 collective-permute-done.12
  698.0 1.0 multiply_reduce_fusion
  699.0 98.4 %psum.47 = f32[]{:T(128)} all-reduce(f32[]{:T(128)} %get-tuple-element.41), channel_id=1, replica_groups=mesh['slab'=8,'sub'=64] {'slab','sub'}, use_global_device_ids=true, to_apply=%region_13.14 | all-reduce | flops 1 | bytes 8 | tf_op jit(solution)/shard_map/psum | solution.py:155
  (91 shorter events, 11.7 us)
Async XLA Ops:
  7.2 184.7 %all-gather.2.cloned.1.call-start = ((), (), s32[]{:S(2)}) async-start(), calls=%async_computation | async-start | bytes 11448320 | tf_op jit(solution)/shard_map/all_gather | solution.py:110
  10.5 135.3 %collective-permute-start = (f32[64,1,98]{2,1,0:T(1,128)S(1)}, f32[64,1,98]{2,1,0:T(1,128)}, u32[]{:S(2)}, u32[]{:S(2)}) collective-permute-start(f32[64,1,98]{2,1,0:T(1,128)S(1)} %get-tuple-element.17), channel_id=1, source_target_pairs={{0,1},{1,2},{2,3},{3,4},{4,5},{5,6},{6,7},{7,8},{8,9},{9,10},{10,1... | collective-permute-start | bytes 75272 | tf_op jit(solution)/shard_map/ppermute | solution.py:22
  14.4 187.9 %collective-permute-start.2 = (f32[64,1,98]{2,1,0:T(1,128)S(1)}, f32[64,1,98]{2,1,0:T(1,128)S(1)}, u32[]{:S(2)}, u32[]{:S(2)}) collective-permute-start(f32[64,1,98]{2,1,0:T(1,128)S(1)} %get-tuple-element.16), channel_id=1, source_target_pairs={{1,0},{2,1},{3,2},{4,3},{5,4},{6,5},{7,6},{8,7},{9,8},{10,9},{11,1... | collective-permute-start | bytes 75272 | tf_op jit(solution)/shard_map/ppermute | solution.py:23
  110.4 6.3 copy-start
  110.4 8.7 %copy-start.1 = (f32[8]{0:T(128)S(1)}, f32[8]{0:T(128)}, u32[]{:S(2)}) copy-start(f32[8]{0:T(128)} %param.8) | copy-start | bytes 100
  119.3 72.5 %copy-start.2 = (f32[8,343]{1,0:T(8,128)S(1)}, f32[8,343]{1,0:T(8,128)}, u32[]{:S(2)}) copy-start(f32[8,343]{1,0:T(8,128)} %param.7) | copy-start | bytes 32932
  200.0 14.4 %collective-permute-start.1 = (f32[1,64]{1,0:T(1,128)S(1)}, f32[1,64]{1,0:T(1,128)S(1)}, u32[]{:S(2)}, u32[]{:S(2)}) collective-permute-start(f32[1,64]{1,0:T(1,128)S(1)} %fusion.60), channel_id=1, source_target_pairs={{0,1},{1,2},{2,3},{3,4},{4,5},{5,6},{6,7},{7,8},{8,9},{9,10},{10,1... | collective-permute-start | bytes 776 | tf_op jit(solution)/shard_map/ppermute | solution.py:22
  202.5 12.6 %collective-permute-start.3 = (f32[1,64]{1,0:T(1,128)S(1)}, f32[1,64]{1,0:T(1,128)S(1)}, u32[]{:S(2)}, u32[]{:S(2)}) collective-permute-start(f32[1,64]{1,0:T(1,128)S(1)} %fusion.60), channel_id=1, source_target_pairs={{1,0},{2,1},{3,2},{4,3},{5,4},{6,5},{7,6},{8,7},{9,8},{10,9},{11,1... | collective-permute-start | bytes 776 | tf_op jit(solution)/shard_map/ppermute | solution.py:23
  216.2 9.4 %collective-permute-start.5 = (f32[1,1,98]{2,1,0:T(1,128)S(1)}, f32[1,1,98]{2,1,0:T(1,128)S(1)}, u32[]{:S(2)}, u32[]{:S(2)}) collective-permute-start(f32[1,1,98]{2,1,0:T(1,128)S(1)} %get-tuple-element.37), channel_id=1, source_target_pairs={{1,0},{2,1},{3,2},{4,3},{5,4},{6,5},{7,6},{8,7},{9,8},{10,9},{11,1... | collective-permute-start | bytes 1184 | tf_op jit(solution)/shard_map/ppermute | solution.py:23
  223.7 8.2 %collective-permute-start.4 = (f32[1,1,98]{2,1,0:T(1,128)S(1)}, f32[1,1,98]{2,1,0:T(1,128)S(1)}, u32[]{:S(2)}, u32[]{:S(2)}) collective-permute-start(f32[1,1,98]{2,1,0:T(1,128)S(1)} %get-tuple-element.36), channel_id=1, source_target_pairs={{0,1},{1,2},{2,3},{3,4},{4,5},{5,6},{6,7},{7,8},{8,9},{9,10},{10,1... | collective-permute-start | bytes 1184 | tf_op jit(solution)/shard_map/ppermute | solution.py:22
  340.7 8.9 %collective-permute-start.6 = (f32[1,64]{1,0:T(1,128)S(1)}, f32[1,64]{1,0:T(1,128)S(1)}, u32[]{:S(2)}, u32[]{:S(2)}) collective-permute-start(f32[1,64]{1,0:T(1,128)S(1)} %fusion.58), channel_id=1, source_target_pairs={{0,1},{1,2},{2,3},{3,4},{4,5},{5,6},{6,7},{7,8},{8,9},{9,10},{10,1... | collective-permute-start | bytes 776 | tf_op jit(solution)/shard_map/ppermute | solution.py:22
  342.6 7.7 collective-permute-start.7
  456.8 5.3 collective-permute-start.9
  459.6 8.2 %collective-permute-start.8 = (f32[1,1,98]{2,1,0:T(1,128)S(1)}, f32[1,1,98]{2,1,0:T(1,128)S(1)}, u32[]{:S(2)}, u32[]{:S(2)}) collective-permute-start(f32[1,1,98]{2,1,0:T(1,128)S(1)} %get-tuple-element.34), channel_id=1, source_target_pairs={{0,1},{1,2},{2,3},{3,4},{4,5},{5,6},{6,7},{7,8},{8,9},{9,10},{10,1... | collective-permute-start | bytes 1184 | tf_op jit(solution)/shard_map/ppermute | solution.py:22
  569.9 8.9 %collective-permute-start.10 = (f32[1,64]{1,0:T(1,128)S(1)}, f32[1,64]{1,0:T(1,128)S(1)}, u32[]{:S(2)}, u32[]{:S(2)}) collective-permute-start(f32[1,64]{1,0:T(1,128)S(1)} %fusion.56), channel_id=1, source_target_pairs={{0,1},{1,2},{2,3},{3,4},{4,5},{5,6},{6,7},{7,8},{8,9},{9,10},{10,1... | collective-permute-start | bytes 776 | tf_op jit(solution)/shard_map/ppermute | solution.py:22
  571.9 7.6 collective-permute-start.11
  686.0 5.6 collective-permute-start.13
  689.7 8.2 %collective-permute-start.12 = (f32[1,1,98]{2,1,0:T(1,128)S(1)}, f32[1,1,98]{2,1,0:T(1,128)S(1)}, u32[]{:S(2)}, u32[]{:S(2)}) collective-permute-start(f32[1,1,98]{2,1,0:T(1,128)S(1)} %get-tuple-element.32), channel_id=1, source_target_pairs={{0,1},{1,2},{2,3},{3,4},{4,5},{5,6},{6,7},{7,8},{8,9},{9,10},{10,1... | collective-permute-start | bytes 1184 | tf_op jit(solution)/shard_map/ppermute | solution.py:22
Sparse Core Ops, SparseCore 0:
  10.9 180.9 all-gather.1
where the time goes:
time: 808 us; the launch traced here: 806 us
  blocking collectives  573 us (71%)
  starting transfers between devices  68.9 us (9%)
  waiting for transfers between devices  65.5 us (8%)
  local copies, waits for them, and re-layouts  28.9 us (4%)
  other arithmetic  28.6 us (4%)
  between operations  21.9 us (3%)
  matrix products  19.7 us (2%)
    psum x3, blocking collectives, residual_inner(): return lax.psum(jnp.sum(residual * precond), ('slab', 'sub'))  312 us
    psum x2, blocking collectives, on_device(): lax.psum(jnp.sum(direction * applied), ('slab', 'sub'))  197 us
    all_gather x1, blocking collectives, on_device(): row_marks = lax.all_gather(marks, 'sub', axis=0, tiled=True)  63.1 us
    ppermute x7, starting transfers between devices, extended_2(): after = lax.ppermute(first, axis, down)  52.4 us
    all_gather x1, waiting for transfers between devices, on_device(): row_values = lax.all_gather(current_values, 'sub', axis=0, tiled=True)  45 us
    ppermute x7, waiting for transfers between devices, extended_2(): before = lax.ppermute(last, axis, up)  18.1 us
    ppermute x7, starting transfers between devices, extended_2(): before = lax.ppermute(last, axis, up)  16.5 us
  transfers between devices with their start and end apart: 15, of which 7 were waited for; matrix products, arithmetic and copies ran while one was open for 8% of the time, Pallas kernels for 0%

commit v1 on v0

v1 whole, which is shorter than its diff:
```python
import functools

import jax
import jax.numpy as jnp
import numpy as np
from jax import lax
from jax.experimental import pallas as pl
from jax.experimental.pallas import tpu as pltpu
from jax.sharding import PartitionSpec as P

BLOCK = 128
CAP = 6
NODES = 343
WIDE = 384
FACE = 49
EL = 8
NB = 64
XN = 4
MARK = 120
SHIFT = 1.0
PENALTY = 10.0
RELAX = 0.2
HIGH = lax.Precision.HIGHEST
F32 = jnp.float32
BF16 = jnp.bfloat16
NT = (((1,), (1,)), ((), ()))
TN = (((0,), (0,)), ((), ()))


def stencil_constants():
    second = np.diag(np.array([1.0, 2, 2, 2, 2, 2, 1]))
    for i in range(6):
        second[i, i + 1] = second[i + 1, i] = -1.0
    one = np.eye(7)
    kel = (
        np.kron(np.kron(second, one), one)
        + np.kron(np.kron(one, second), one)
        + np.kron(one, np.kron(one, second))
    )
    full = np.zeros((WIDE, WIDE), np.float32)
    full[:NODES, :NODES] = kel
    return full, np.diagonal(full)


def split2(value):
    hi = value.astype(BF16)
    lo = (value - hi.astype(F32)).astype(BF16)
    return hi, lo


def iota(shape, dim):
    return lax.broadcasted_iota(jnp.int32, shape, dim)


def dot(a, b, dims=(((1,), (0,)), ((), ())), precision=None):
    return lax.dot_general(a, b, dims, precision=precision, preferred_element_type=F32)


def kernel(
    slabs,
    subs,
    cond_ref,
    count_ref,
    src_ref,
    basis_ref,
    vals_ref,
    elem_ref,
    own_ref,
    kel_ref,
    kdiag_ref,
    x_out,
    r_out,
    vext,
    a_src,
    a_dst,
    b_src,
    b_dst,
    bt_ref,
    cz_ref,
    padded,
    source_ref,
    g_src,
    g_dst,
    f_src,
    f_dst,
    s_src,
    s_dst,
    a_sem,
    b_sem,
    g_sem,
    f_sem,
    s_sem,
):
    zn = subs // XN
    total = slabs * subs
    slab = lax.axis_index("slab")
    sub = lax.axis_index("sub")
    x = lax.rem(sub, XN)
    z = lax.div(sub, XN)
    chain = slab * subs + sub
    rows = vals_ref.shape[0]
    slot = zn * CAP

    def x_peer(i):
        return (slab, z * XN + lax.rem(x + i, XN))

    def z_peer(i):
        return (slab, lax.rem(z + i, zn) * XN + x)

    def slab_peer(i):
        return (lax.rem(slab + i, slabs), sub)

    def chain_peer(step):
        other = lax.rem(chain + step + total, total)
        return (lax.div(other, subs), lax.rem(other, subs))

    peers = (
        [x_peer(i) for i in range(1, XN)]
        + [z_peer(i) for i in range(1, zn)]
        + [slab_peer(i) for i in range(1, slabs)]
        + [chain_peer(step) for step in (-1, 1, -2, 2)]
    )
    barrier = pltpu.get_barrier_semaphore()
    for peer in peers:
        pl.semaphore_signal(
            barrier, inc=1, device_id=peer, device_id_type=pl.DeviceIdType.MESH
        )

    def send(src, dst, sems, k, peer):
        copy = pltpu.make_async_remote_copy(
            src_ref=src,
            dst_ref=dst,
            send_sem=sems.at[0, k],
            recv_sem=sems.at[1, k],
            device_id=peer,
            device_id_type=pl.DeviceIdType.MESH,
        )
        copy.start()
        return copy

    order = iota((subs, rows), 0)
    order = lax.rem(order, zn) * XN + lax.div(order, zn)
    live = lax.div(iota((subs, rows), 1), BLOCK) < count_ref[0]
    owned = ((own_ref[...] == order) & live).astype(F32)
    before = (iota((rows, rows), 0) < iota((rows, rows), 1)).astype(BF16)
    rank = dot(owned.astype(BF16), before)
    pieces = []
    for to in range(XN):
        mine = owned[to * zn : (to + 1) * zn]
        place = rank[to * zn : (to + 1) * zn]
        for j in range(CAP):
            pieces.append(jnp.where(place == float(j), mine, 0.0))
    select = jnp.concatenate(pieces, axis=0).astype(BF16)
    vext[:, 256:] = jnp.zeros((rows, 128), BF16)
    vext[:, :NODES] = vals_ref[...]
    marks = (elem_ref[...] == iota((128, rows), 0) - MARK).astype(BF16)
    moved = dot(select, vext[...])
    marked = dot(select, marks, NT)
    a_src[:, :, :256] = moved[:, :256].astype(BF16).reshape(XN, slot, 256)
    a_src[:, :, 256:] = (moved[:, 256:] + marked).astype(BF16).reshape(XN, slot, 128)

    pl.semaphore_wait(barrier, len(peers))
    a_copies = [
        send(a_src.at[lax.rem(x + i, XN)], a_dst.at[i], a_sem, i, x_peer(i))
        for i in range(1, XN)
    ]
    a_dst[0] = a_src[x]

    lane = iota((1, WIDE), 1)
    left = lane < FACE
    right = (lane >= NODES - FACE) & (lane < NODES)
    facew = jnp.where(left | right, PENALTY, 0.0)
    flat = basis_ref[...].reshape(NB * EL, NODES)
    padded[2] = jnp.zeros((NB * EL, 128), F32)
    padded[0] = flat[:, 0:128]
    padded[1] = flat[:, 128:256]
    padded[2, :, : NODES - 256] = flat[:, 256:]
    for t in range(3):
        for e in range(EL):
            at = e * WIDE + t * 128
            bt_ref[:, at : at + 128] = padded[t, pl.ds(e, NB, stride=EL), :]

    def element(ref, e):
        return ref[:, e * WIDE : (e + 1) * WIDE]

    kel = kel_ref[...]
    applied = []
    for e in range(EL):
        be = element(bt_ref, e)
        hi, lo = split2(be)
        stiff = dot(hi, kel) + dot(lo, kel)
        out = cond_ref[e] * stiff + (RELAX + facew) * be
        if e > 0:
            turned = pltpu.roll(element(bt_ref, e - 1), WIDE - NODES + FACE, 1)
            out = out - jnp.where(left, PENALTY * turned, 0.0)
        if e < EL - 1:
            turned = pltpu.roll(element(bt_ref, e + 1), NODES - FACE, 1)
            out = out - jnp.where(right, PENALTY * turned, 0.0)
        applied.append(out)
    matrix = dot(bt_ref[...], jnp.concatenate(applied, axis=1), NT, HIGH)

    for copy in a_copies:
        copy.wait()
    arrived = a_dst[...].reshape(XN * slot, WIDE)
    spread = (iota((128, 128), 0) == MARK + lax.rem(iota((128, 128), 1), EL)).astype(BF16)
    spread = dot(arrived[:, 256:], spread)
    keep = lax.rem(iota(spread.shape, 0), zn) == lax.div(iota(spread.shape, 1), EL)
    weights = jnp.where(keep, spread, 0.0)
    sums = dot(weights.T.astype(BF16), arrived)
    b_src[...] = sums[: zn * EL].reshape(zn, EL, WIDE)
    b_copies = [
        send(b_src.at[lax.rem(z + i, zn)], b_dst.at[i], b_sem, i, z_peer(i))
        for i in range(1, zn)
    ]
    b_dst[0] = b_src[z]

    unit = (iota((NB, NB), 0) == iota((NB, NB), 1)).astype(F32)
    work = jnp.concatenate([matrix, unit], axis=1)
    row_id = iota((NB, 2 * NB), 0)
    for k in range(NB):
        row = work[k : k + 1, :] / work[k : k + 1, k : k + 1]
        work = jnp.where(row_id == k, row, work - work[:, k : k + 1] * row)
    inverse = work[:, NB:]
    cz_ref[...] = dot(inverse, bt_ref[...], precision=HIGH)

    low = iota((1, 128), 1)
    near = low < FACE

    def left_face(value):
        return jnp.where(near, value[:, 0:128], 0.0)

    def right_face(value):
        return jnp.where(near, pltpu.roll(value[:, 256:WIDE], 128 - 38, 1), 0.0)

    w = PENALTY * (
        left_face(element(cz_ref, 0))
        + pltpu.roll(right_face(element(cz_ref, EL - 1)), 64, 1)
    )
    face_l = left_face(element(bt_ref, 0))
    face_r = right_face(element(bt_ref, EL - 1))
    g_src[0] = dot(face_l.T, w, precision=HIGH)[:56]
    g_src[1] = dot(face_r.T, w, precision=HIGH)[:56]
    g_copies = [
        send(g_src.at[0], g_dst.at[0], g_sem, 0, chain_peer(-1)),
        send(g_src.at[1], g_dst.at[1], g_sem, 1, chain_peer(1)),
    ]

    el_row = iota((EL, WIDE), 0)
    conduct = jnp.zeros((EL, WIDE), F32)
    for e in range(EL):
        conduct = jnp.where(el_row == e, cond_ref[e], conduct)
    diagonal = conduct * kdiag_ref[...] + RELAX + facew
    inner_lane = iota((EL, WIDE), 1) < NODES
    source_ref[:, 256:] = jnp.zeros((EL, 128), F32)
    source_ref[:, :NODES] = src_ref[...]
    for copy in b_copies:
        copy.wait()
    currents = b_dst[0]
    for i in range(1, zn):
        currents = currents + b_dst[i]
    rhs = source_ref[...] + jnp.where(inner_lane, currents, 0.0)

    has = {step: (chain + step >= 0) & (chain + step < total) for step in (-2, -1, 1, 2)}
    eye = iota((56, 128), 0) == iota((56, 128), 1)

    def turn(matrix, vector):
        column = jnp.sum(matrix * vector, axis=1, keepdims=True)
        return jnp.sum(jnp.where(eye, column, 0.0), axis=0, keepdims=True)

    def lift(column):
        line = jnp.sum(bt_ref[...] * column, axis=0, keepdims=True)
        return jnp.concatenate(
            [line[:, e * WIDE : (e + 1) * WIDE] for e in range(EL)], axis=0
        )

    def gram(a, b):
        prod = a * b
        prod = prod[:, 0:128] + prod[:, 128:256] + prod[:, 256:384]
        return jnp.sum(prod, axis=0, keepdims=True)

    pad_row = jnp.zeros((1, 256), F32)
    residuals, preconds = [rhs], []
    products = {}
    all_copies = []
    for k in range(3):
        res = residuals[k]
        scaled = res / diagonal
        acc = jnp.zeros((NB, WIDE), F32)
        for e in range(EL):
            acc = acc + element(cz_ref, e) * res[e : e + 1, :]
        acc = acc[:, 0:128] + acc[:, 128:256] + acc[:, 256:384]
        first = lift(jnp.sum(acc, axis=1, keepdims=True))
        fl = left_face(first[0:1])
        fr = right_face(first[EL - 1 : EL])
        el = left_face(scaled[0:1]) + fl
        er = right_face(scaled[EL - 1 : EL]) + fr
        f_src[k] = jnp.concatenate([fl, fr, el, er, jnp.zeros((4, 128), F32)], axis=0)
        copies = [
            send(f_src.at[k], f_dst.at[k, i], f_sem, 4 * k + i, chain_peer(step))
            for i, step in enumerate((-1, 1, -2, 2))
        ]
        for i in range(k + 1):
            for j in range(k):
                if (i, j) not in products:
                    products[i, j] = gram(residuals[i], preconds[j])
        partial = scaled + first
        if k == 0:
            for copy in g_copies:
                copy.wait()
        for copy in copies:
            copy.wait()
        after1 = jnp.where(has[1], f_dst[k, 0], 0.0)
        before1 = jnp.where(has[-1], f_dst[k, 1], 0.0)
        after2 = jnp.where(has[2], f_dst[k, 2], 0.0)
        before2 = jnp.where(has[-2], f_dst[k, 3], 0.0)
        own_v = before1[1:2] + pltpu.roll(after1[0:1], 64, 1)
        after_v = fr + pltpu.roll(after2[0:1], 64, 1)
        before_v = before2[1:2] + pltpu.roll(fl, 64, 1)
        pre = partial + lift(jnp.sum(w * own_v, axis=1, keepdims=True))
        after_face = jnp.where(has[1], after1[2:3] + turn(g_dst[0], after_v), 0.0)
        before_face = jnp.where(has[-1], before1[3:4] + turn(g_dst[1], before_v), 0.0)
        hi, lo = split2(pre)
        both = jnp.concatenate([hi.astype(F32), lo.astype(F32)], axis=0).astype(BF16)
        stiff = dot(both, kel)
        stiff = stiff[0:EL] + stiff[EL : 2 * EL]
        from_left = pltpu.roll(pltpu.roll(pre, 1, 0), WIDE - NODES + FACE, 1)
        from_left = jnp.where(
            el_row == 0, jnp.concatenate([before_face, pad_row], axis=1), from_left
        )
        from_right = pltpu.roll(pltpu.roll(pre, EL - 1, 0), NODES - FACE, 1)
        from_right = jnp.where(
            el_row == EL - 1,
            jnp.concatenate([pad_row, pltpu.roll(after_face, 38, 1)], axis=1),
            from_right,
        )
        image = conduct * stiff + (RELAX + facew) * pre
        image = image - PENALTY * (
            jnp.where(left, from_left, 0.0) + jnp.where(right, from_right, 0.0)
        )
        preconds.append(pre)
        residuals.append(image - SHIFT * res)

    for i in range(4):
        for j in range(3):
            if (i, j) not in products:
                products[i, j] = gram(residuals[i], preconds[j])
    share = jnp.concatenate(
        [products[i, j] for i in range(4) for j in range(3)] + [jnp.zeros((4, 128), F32)], axis=0
    )
    at = 0
    for stage, (count, peer) in enumerate(((XN, x_peer), (zn, z_peer), (slabs, slab_peer))):
        s_src[stage] = share
        copies = [
            send(s_src.at[stage], s_dst.at[at + i - 1], s_sem, at + i - 1, peer(i))
            for i in range(1, count)
        ]
        for copy in copies:
            copy.wait()
        for i in range(1, count):
            share = share + s_dst[at + i - 1]
        at += count - 1

    sums = jnp.sum(share, axis=1, keepdims=True)
    n = [[sums[3 * i + j : 3 * i + j + 1] for j in range(3)] for i in range(4)]

    def form(p, q):
        value = 0.0
        for i, a in enumerate(p):
            line = 0.0
            for j, b in enumerate(q):
                line = line + n[i][j] * b
            value = value + a * line
        return value

    zero = jnp.zeros((1, 1), F32)
    one = jnp.ones((1, 1), F32)
    res_c = [one]
    dir_c = [one]
    sol_c = [zero, zero, zero]
    inner = form(res_c, res_c)
    for k in range(3):
        image_c = [zero] + dir_c
        image_c = [v + SHIFT * u for v, u in zip(image_c, dir_c + [zero])]
        step = inner / form(image_c, dir_c)
        for j, v in enumerate(dir_c):
            sol_c[j] = sol_c[j] + step * v
        res_c = [u - step * v for u, v in zip(res_c + [zero], image_c)]
        if k < 2:
            fresh = form(res_c, res_c)
            ratio = fresh / inner
            dir_c = [u + ratio * v for u, v in zip(res_c, dir_c + [zero])]
            inner = fresh
    answer = sum(sol_c[j] * preconds[j] for j in range(3))
    remain = sum(res_c[j] * residuals[j] for j in range(4))
    x_out[...] = answer[:, :NODES]
    r_out[...] = remain[:, :NODES]


def on_device(slabs, subs, source, conductivity, basis, values, elements, owners, counts):
    rows = values.shape[0]
    zn = subs // XN
    kel, kdiag = stencil_constants()
    vmem = pl.BlockSpec(memory_space=pltpu.VMEM)
    smem = pl.BlockSpec(memory_space=pltpu.SMEM)
    slot = zn * CAP
    peers = XN + zn + slabs - 3
    dma = pltpu.SemaphoreType.DMA
    out = jax.ShapeDtypeStruct(source.shape, F32)
    return pl.pallas_call(
        functools.partial(kernel, slabs, subs),
        out_shape=(out, out),
        in_specs=[smem, smem] + [vmem] * 7,
        out_specs=(vmem, vmem),
        scratch_shapes=[
            pltpu.VMEM((rows, WIDE), BF16),
            pltpu.VMEM((XN, slot, WIDE), BF16),
            pltpu.VMEM((XN, slot, WIDE), BF16),
            pltpu.VMEM((zn, EL, WIDE), F32),
            pltpu.VMEM((zn, EL, WIDE), F32),
            pltpu.VMEM((NB, EL * WIDE), F32),
            pltpu.VMEM((NB, EL * WIDE), F32),
            pltpu.VMEM((3, NB * EL, 128), F32),
            pltpu.VMEM((EL, WIDE), F32),
            pltpu.VMEM((2, 56, 128), F32),
            pltpu.VMEM((2, 56, 128), F32),
            pltpu.VMEM((3, 8, 128), F32),
            pltpu.VMEM((3, 4, 8, 128), F32),
            pltpu.VMEM((3, 16, 128), F32),
            pltpu.VMEM((peers, 16, 128), F32),
            dma((2, XN)),
            dma((2, zn)),
            dma((2, 2)),
            dma((2, 12)),
            dma((2, peers)),
        ],
        compiler_params=pltpu.CompilerParams(
            collective_id=0, has_side_effects=True, vmem_limit_bytes=48 * 1024 * 1024
        ),
    )(
        conductivity,
        counts,
        source,
        basis,
        values,
        elements.reshape(1, rows),
        owners.reshape(1, rows),
        jnp.asarray(kel, BF16),
        jnp.asarray(kdiag.reshape(1, WIDE)),
    )


def solution(mesh):
    both = ("slab", "sub")
    placed = (
        P(both, None),
        P(both),
        P(None, both, None),
        P(both, None),
        P(both),
        P(both, None),
        P(both),
    )
    return jax.shard_map(
        functools.partial(on_device, mesh.shape["slab"], mesh.shape["sub"]),
        mesh=mesh,
        in_specs=placed,
        out_specs=(P(both, None), P(both, None)),
        check_vma=False,
    )
```

time: 808 us -> 79.9 us (0.10)
  blocking collectives: 573 us -> 0 us
  Pallas kernels: 0 us -> 74.8 us
  starting transfers between devices: 68.9 us -> 0 us
  waiting for transfers between devices: 65.5 us -> 0 us
  other arithmetic: 28.6 us -> 0 us
  local copies, waits for them, and re-layouts: 28.9 us -> 3.47 us
  between operations: 21.9 us -> 1.44 us
  matrix products: 19.7 us -> 0 us
    psum x5 -> x0, blocking collectives: 509 us -> none  [the longest x3 312 us: residual_inner(): return lax.psum(jnp.sum(residual * precond), ('slab', 'sub'))]
    pallas_call x0 -> x1, Pallas kernels: none -> 74.8 us  [on_device(): pl.pallas_call(functools.partial(kernel, slabs, subs), out_shape=(out, ou...]
    ppermute x14 -> x0, starting transfers between devices: 68.9 us -> none  [the longest x7 52.4 us: extended_2(): after = lax.ppermute(first, axis, down)]
    all_gather x1 -> x0, blocking collectives: 63.1 us -> none  [on_device(): row_marks = lax.all_gather(marks, 'sub', axis=0, tiled=True)]
    all_gather x1 -> x0, waiting for transfers between devices: 45 us -> none  [on_device(): row_values = lax.all_gather(current_values, 'sub', axis=0, tiled=True)]
    ppermute x14 -> x0, waiting for transfers between devices: 19.8 us -> none  [the longest x7 18.1 us: extended_2(): before = lax.ppermute(last, axis, up)]
    dot_general x27 -> x0, matrix products: 19.5 us -> none  [the longest x1 7.21 us: on_device(): jnp.dot(select.astype(jnp.bfloat16), row_values, preferred_element_type=j...]
    another operation x8 -> x0, other arithmetic: 13.5 us -> none  [the longest x3 6.52 us: invert(): factor = jnp.linalg.cholesky(matrix)]
  transfers between devices with their start and end apart: 15 -> 0, of which waited for: 7 -> 0; matrix products, arithmetic and copies ran while one was open for 8% -> 0% of each run, Pallas kernels for 0% -> 0%
where the time goes in v1:
time: 79.9 us; the launch traced here: 79.7 us
  Pallas kernels  74.8 us (94%)
  local copies, waits for them, and re-layouts  3.47 us (4%)
  between operations  1.44 us (2%)
    pallas_call x1, Pallas kernels, on_device(): pl.pallas_call(functools.partial(kernel, slabs, subs), out_shape=(out, ou...  74.8 us
    unnamed x17, local copies, waits for them, and re-layouts  3.47 us

profile of v1, /device:TPU:1, one launch (start us, length us, event | category | flops | bytes accessed | tf_op | source)
XLA Modules:
  0.0 79.7 jit_solution(6220322233586410412)
XLA Ops:
  0.6 0.0 copy-start.1
  1.3 0.0 copy-start.2
  1.3 0.0 copy-start.3
  1.4 0.0 copy-start.4
  1.4 0.0 copy-start.5
  1.4 0.0 copy-start.6
  1.4 1.1 %copy.11.vals_ref = bf16[256,343]{1,0:T(8,128)(2,1)S(1)} copy(bf16[256,343]{0,1:T(8,128)(2,1)} %param.12) | data formatting | bytes 351232 | tf_op args[3]
  2.5 0.0 copy-done.1
  2.5 0.0 copy-done.2
  2.5 0.0 copy-done.3
  2.5 0.0 copy-done.4
  2.5 0.0 copy-done.5
  2.6 0.0 copy-done.6
  2.6 0.0 copy-start
  2.6 1.1 %copy-done = f32[64,8,343]{2,1,0:T(8,128)S(1)} copy-done((f32[64,8,343]{2,1,0:T(8,128)S(1)}, f32[64,8,343]{2,1,0:T(8,128)}, u32[]{:S(2)}) %copy-start) | copy-done | bytes 702488
  3.7 74.8 %shard_map.104 = (f32[8,343]{1,0:T(8,128)S(1)}, f32[8,343]{1,0:T(8,128)S(1)}) custom-call(f32[8]{0:T(128)S(1)} %copy-done.6, s32[1]{0:T(128)S(6)} %copy.14.count_ref, f32[8,343]{1,0:T(8,128)S(1)} %copy-done.2, f32[64,8,343]{2,1,0:T(8,128)S(1)} %copy-done, bf16[256,343]{1,0:T(8,128)(2,1)S(1)} %copy.11.vals_ref, s32[1,256]{1,0:T(1,128)S(1)} %bitcast.2, ...), custom_call_target="tpu_custom_call" | custom-call | tf_op jit(solution)/shard_map/pallas_call | solution.py:409
  78.5 0.6 copy.15
  79.1 0.6 copy.16
Async XLA Ops:
  0.6 1.9 %copy-start.1 = (bf16[384,384]{1,0:T(8,128)(2,1)S(1)}, bf16[384,384]{1,0:T(8,128)(2,1)}, u32[]{:S(2)}) copy-start(bf16[384,384]{1,0:T(8,128)(2,1)} %constant.4.clone.kel_ref) | copy-start | bytes 884740
  1.3 1.2 %copy-start.2 = (f32[8,343]{1,0:T(8,128)S(1)}, f32[8,343]{1,0:T(8,128)}, u32[]{:S(2)}) copy-start(f32[8,343]{1,0:T(8,128)} %src_ref.1) | copy-start | bytes 32932
  1.3 1.2 %copy-start.3 = (f32[1,384]{1,0:T(1,128)S(1)}, f32[1,384]{1,0:T(1,128)}, u32[]{:S(2)}) copy-start(f32[1,384]{1,0:T(1,128)} %constant.5.clone.kdiag_ref) | copy-start | bytes 4612
  1.4 1.2 %copy-start.4 = (s32[256]{0:T(256)S(1)}, s32[256]{0:T(256)}, u32[]{:S(2)}) copy-start(s32[256]{0:T(256)} %param.13) | copy-start | bytes 3076
  1.4 1.2 %copy-start.5 = (s32[256,1]{0,1:T(1,128)S(1)}, s32[256,1]{0,1:T(1,128)}, u32[]{:S(2)}) copy-start(s32[256,1]{0,1:T(1,128)} %param.14) | copy-start | bytes 3076
  1.4 1.2 %copy-start.6 = (f32[8]{0:T(128)S(1)}, f32[8]{0:T(128)}, u32[]{:S(2)}) copy-start(f32[8]{0:T(128)} %cond_ref.1) | copy-start | bytes 100
  2.6 1.1 %copy-start = (f32[64,8,343]{2,1,0:T(8,128)S(1)}, f32[64,8,343]{2,1,0:T(8,128)}, u32[]{:S(2)}) copy-start(f32[64,8,343]{2,1,0:T(8,128)} %basis_ref.1) | copy-start | bytes 2107396

commit v2 on v1

--- a/solution.py
+++ b/solution.py
@@ -39,7 +39,8 @@
     )
     full = np.zeros((WIDE, WIDE), np.float32)
     full[:NODES, :NODES] = kel
-    return full, np.diagonal(full)
+    full[NODES + 1] = np.diagonal(full)
+    return full
 
 
 def split2(value):
@@ -67,10 +68,16 @@
     elem_ref,
     own_ref,
     kel_ref,
-    kdiag_ref,
     x_out,
     r_out,
-    vext,
+    cond_in,
+    count_in,
+    src_in,
+    basis_in,
+    vals_in,
+    elem_in,
+    own_in,
+    kel_in,
     a_src,
     a_dst,
     b_src,
@@ -90,6 +97,7 @@
     g_sem,
     f_sem,
     s_sem,
+    in_sem,
 ):
     zn = subs // XN
     total = slabs * subs
@@ -98,7 +106,7 @@
     x = lax.rem(sub, XN)
     z = lax.div(sub, XN)
     chain = slab * subs + sub
-    rows = vals_ref.shape[0]
+    rows = vals_ref.shape[1]
     slot = zn * CAP
 
     def x_peer(i):
@@ -107,18 +115,25 @@
     def z_peer(i):
         return (slab, lax.rem(z + i, zn) * XN + x)
 
-    def slab_peer(i):
-        return (lax.rem(slab + i, slabs), sub)
+    def plane_peer(i, j):
+        return (lax.rem(slab + 2 * j, slabs), z * XN + lax.rem(x + i, XN))
+
+    core_peer = (slab + 1 - 2 * lax.rem(slab, 2), sub)
+    ys = slabs // 2
+    far = sorted(range(1, zn), key=lambda i: -min(i, zn - i))
+    plane = [(i, j) for i in range(XN) for j in range(ys) if i or j]
+    plane.sort(key=lambda p: -min(p[0], XN - p[0]) - min(p[1], ys - p[1]))
+    x_order = sorted(range(1, XN), key=lambda i: -min(i, XN - i))
 
     def chain_peer(step):
         other = lax.rem(chain + step + total, total)
         return (lax.div(other, subs), lax.rem(other, subs))
 
     peers = (
-        [x_peer(i) for i in range(1, XN)]
-        + [z_peer(i) for i in range(1, zn)]
-        + [slab_peer(i) for i in range(1, slabs)]
-        + [chain_peer(step) for step in (-1, 1, -2, 2)]
+        [z_peer(i) for i in far]
+        + [chain_peer(step) for step in (-2, 2, -1, 1)]
+        + [plane_peer(i, j) for i, j in plane]
+        + [core_peer]
     )
     barrier = pltpu.get_barrier_semaphore()
     for peer in peers:
@@ -138,10 +153,30 @@
         copy.start()
         return copy
 
+    fetches = [
+        pltpu.make_async_copy(src, dst, in_sem.at[k])
+        for k, (src, dst) in enumerate(
+            (
+                (own_ref, own_in),
+                (count_ref, count_in),
+                (elem_ref, elem_in),
+                (vals_ref, vals_in),
+                (basis_ref, basis_in),
+                (kel_ref, kel_in),
+                (cond_ref, cond_in),
+                (src_ref, src_in),
+            )
+        )
+    ]
+    for fetch in fetches:
+        fetch.start()
+
+    for fetch in fetches[:4]:
+        fetch.wait()
     order = iota((subs, rows), 0)
     order = lax.rem(order, zn) * XN + lax.div(order, zn)
-    live = lax.div(iota((subs, rows), 1), BLOCK) < count_ref[0]
-    owned = ((own_ref[...] == order) & live).astype(F32)
+    live = lax.div(iota((subs, rows), 1), BLOCK) < count_in[0]
+    owned = ((own_in[...] == order) & live).astype(F32)
     before = (iota((rows, rows), 0) < iota((rows, rows), 1)).astype(BF16)
     rank = dot(owned.astype(BF16), before)
     pieces = []
@@ -151,26 +186,27 @@
         for j in range(CAP):
             pieces.append(jnp.where(place == float(j), mine, 0.0))
     select = jnp.concatenate(pieces, axis=0).astype(BF16)
-    vext[:, 256:] = jnp.zeros((rows, 128), BF16)
-    vext[:, :NODES] = vals_ref[...]
-    marks = (elem_ref[...] == iota((128, rows), 0) - MARK).astype(BF16)
-    moved = dot(select, vext[...])
-    marked = dot(select, marks, NT)
-    a_src[:, :, :256] = moved[:, :256].astype(BF16).reshape(XN, slot, 256)
-    a_src[:, :, 256:] = (moved[:, 256:] + marked).astype(BF16).reshape(XN, slot, 128)
+    marks = (elem_in[...] == iota((128, rows), 0) - MARK).astype(BF16)
+    moved = dot(select, vals_in[...], NT).astype(BF16)
+    marked = dot(select, marks, NT).astype(BF16)
+    a_src[:, :, :256] = moved[:, :256].reshape(XN, slot, 256)
+    a_src[:, :, 256:] = marked.reshape(XN, slot, 128)
+    a_src[:, :, 256:NODES] = moved[:, 256:].reshape(XN, slot, NODES - 256)
 
     pl.semaphore_wait(barrier, len(peers))
     a_copies = [
         send(a_src.at[lax.rem(x + i, XN)], a_dst.at[i], a_sem, i, x_peer(i))
-        for i in range(1, XN)
+        for i in x_order
     ]
     a_dst[0] = a_src[x]
 
+    for fetch in fetches[4:]:
+        fetch.wait()
     lane = iota((1, WIDE), 1)
     left = lane < FACE
     right = (lane >= NODES - FACE) & (lane < NODES)
     facew = jnp.where(left | right, PENALTY, 0.0)
-    flat = basis_ref[...].reshape(NB * EL, NODES)
+    flat = basis_in[...].reshape(NB * EL, NODES)
     padded[2] = jnp.zeros((NB * EL, 128), F32)
     padded[0] = flat[:, 0:128]
     padded[1] = flat[:, 128:256]
@@ -183,13 +219,13 @@
     def element(ref, e):
         return ref[:, e * WIDE : (e + 1) * WIDE]
 
-    kel = kel_ref[...]
+    kel = kel_in[...]
     applied = []
     for e in range(EL):
         be = element(bt_ref, e)
         hi, lo = split2(be)
         stiff = dot(hi, kel) + dot(lo, kel)
-        out = cond_ref[e] * stiff + (RELAX + facew) * be
+        out = cond_in[e] * stiff + (RELAX + facew) * be
         if e > 0:
             turned = pltpu.roll(element(bt_ref, e - 1), WIDE - NODES + FACE, 1)
             out = out - jnp.where(left, PENALTY * turned, 0.0)
@@ -210,7 +246,7 @@
     b_src[...] = sums[: zn * EL].reshape(zn, EL, WIDE)
     b_copies = [
         send(b_src.at[lax.rem(z + i, zn)], b_dst.at[i], b_sem, i, z_peer(i))
-        for i in range(1, zn)
+        for i in far
     ]
     b_dst[0] = b_src[z]
 
@@ -248,11 +284,12 @@
     el_row = iota((EL, WIDE), 0)
     conduct = jnp.zeros((EL, WIDE), F32)
     for e in range(EL):
-        conduct = jnp.where(el_row == e, cond_ref[e], conduct)
-    diagonal = conduct * kdiag_ref[...] + RELAX + facew
+        conduct = jnp.where(el_row == e, cond_in[e], conduct)
+    kdiag = kel_in[NODES - 7 : NODES + 9].astype(F32)[8:9]
+    diagonal = conduct * kdiag + RELAX + facew
     inner_lane = iota((EL, WIDE), 1) < NODES
     source_ref[:, 256:] = jnp.zeros((EL, 128), F32)
-    source_ref[:, :NODES] = src_ref[...]
+    source_ref[:, :NODES] = src_in[...]
     for copy in b_copies:
         copy.wait()
     currents = b_dst[0]
@@ -297,7 +334,7 @@
         f_src[k] = jnp.concatenate([fl, fr, el, er, jnp.zeros((4, 128), F32)], axis=0)
         copies = [
             send(f_src.at[k], f_dst.at[k, i], f_sem, 4 * k + i, chain_peer(step))
-            for i, step in enumerate((-1, 1, -2, 2))
+            for i, step in ((2, -2), (3, 2), (0, -1), (1, 1))
         ]
         for i in range(k + 1):
             for j in range(k):
@@ -347,20 +384,34 @@
     share = jnp.concatenate(
         [products[i, j] for i in range(4) for j in range(3)] + [jnp.zeros((4, 128), F32)], axis=0
     )
+    half = iota((8, 128), 1) < 64
+    share = share + pltpu.roll(share, 64, 1)
+    share = jnp.where(half, share[0:8], share[8:16])
     at = 0
-    for stage, (count, peer) in enumerate(((XN, x_peer), (zn, z_peer), (slabs, slab_peer))):
+    stages = (
+        [core_peer],
+        [plane_peer(i, j) for i, j in plane],
+        [z_peer(i) for i in far],
+    )
+    for stage, to in enumerate(stages):
         s_src[stage] = share
         copies = [
-            send(s_src.at[stage], s_dst.at[at + i - 1], s_sem, at + i - 1, peer(i))
-            for i in range(1, count)
+            send(s_src.at[stage], s_dst.at[at + i], s_sem, at + i, peer)
+            for i, peer in enumerate(to)
         ]
         for copy in copies:
             copy.wait()
-        for i in range(1, count):
-            share = share + s_dst[at + i - 1]
-        at += count - 1
-
-    sums = jnp.sum(share, axis=1, keepdims=True)
+        for i in range(len(to)):
+            share = share + s_dst[at + i]
+        at += len(to)
+
+    sums = jnp.concatenate(
+        [
+            jnp.sum(jnp.where(half, share, 0.0), axis=1, keepdims=True),
+            jnp.sum(jnp.where(half, 0.0, share), axis=1, keepdims=True),
+        ],
+        axis=0,
+    )
     n = [[sums[3 * i + j : 3 * i + j + 1] for j in range(3)] for i in range(4)]
 
     def form(p, q):
@@ -399,20 +450,27 @@
 def on_device(slabs, subs, source, conductivity, basis, values, elements, owners, counts):
     rows = values.shape[0]
     zn = subs // XN
-    kel, kdiag = stencil_constants()
+    kel = stencil_constants()
     vmem = pl.BlockSpec(memory_space=pltpu.VMEM)
-    smem = pl.BlockSpec(memory_space=pltpu.SMEM)
+    hbm = pl.BlockSpec(memory_space=pltpu.HBM)
     slot = zn * CAP
-    peers = XN + zn + slabs - 3
+    peers = XN * (slabs // 2) - 1 + 1 + zn - 1
     dma = pltpu.SemaphoreType.DMA
     out = jax.ShapeDtypeStruct(source.shape, F32)
     return pl.pallas_call(
         functools.partial(kernel, slabs, subs),
         out_shape=(out, out),
-        in_specs=[smem, smem] + [vmem] * 7,
+        in_specs=[hbm] * 8,
         out_specs=(vmem, vmem),
         scratch_shapes=[
-            pltpu.VMEM((rows, WIDE), BF16),
+            pltpu.SMEM((EL,), F32),
+            pltpu.SMEM((1,), jnp.int32),
+            pltpu.VMEM((EL, NODES), F32),
+            pltpu.VMEM((NB, EL, NODES), F32),
+            pltpu.VMEM((NODES, rows), BF16),
+            pltpu.VMEM((1, rows), jnp.int32),
+            pltpu.VMEM((1, rows), jnp.int32),
+            pltpu.VMEM((WIDE, WIDE), BF16),
             pltpu.VMEM((XN, slot, WIDE), BF16),
             pltpu.VMEM((XN, slot, WIDE), BF16),
             pltpu.VMEM((zn, EL, WIDE), F32),
@@ -425,27 +483,27 @@
             pltpu.VMEM((2, 56, 128), F32),
             pltpu.VMEM((3, 8, 128), F32),
             pltpu.VMEM((3, 4, 8, 128), F32),
-            pltpu.VMEM((3, 16, 128), F32),
-            pltpu.VMEM((peers, 16, 128), F32),
+            pltpu.VMEM((3, 8, 128), F32),
+            pltpu.VMEM((peers, 8, 128), F32),
             dma((2, XN)),
             dma((2, zn)),
             dma((2, 2)),
             dma((2, 12)),
             dma((2, peers)),
+            dma((8,)),
         ],
         compiler_params=pltpu.CompilerParams(
-            collective_id=0, has_side_effects=True, vmem_limit_bytes=48 * 1024 * 1024
+            collective_id=0, has_side_effects=True, vmem_limit_bytes=60 * 1024 * 1024
         ),
     )(
         conductivity,
         counts,
         source,
         basis,
-        values,
+        values.T,
         elements.reshape(1, rows),
         owners.reshape(1, rows),
         jnp.asarray(kel, BF16),
-        jnp.asarray(kdiag.reshape(1, WIDE)),
     )
 
 

time: 79.9 us -> 73.3 us (0.917)
  Pallas kernels: 74.8 us -> 69.9 us
  local copies, waits for them, and re-layouts: 3.47 us -> 1.92 us
    pallas_call x1, Pallas kernels: 74.8 us -> 69.9 us  [on_device(): pl.pallas_call(functools.partial(kernel, slabs, subs), out_shape=(out, ou...]
    unnamed x17 -> x4, local copies, waits for them, and re-layouts: 3.47 us -> 1.92 us
where the time goes in v2:
time: 73.3 us; the launch traced here: 73.1 us
  Pallas kernels  69.9 us (95%)
  local copies, waits for them, and re-layouts  1.92 us (3%)
  between operations  1.3 us (2%)
    pallas_call x1, Pallas kernels, on_device(): pl.pallas_call(functools.partial(kernel, slabs, subs), out_shape=(out, ou...  69.9 us
    unnamed x4, local copies, waits for them, and re-layouts  1.92 us

profile of v2, /device:TPU:1, one launch (start us, length us, event | category | flops | bytes accessed | tf_op | source)
XLA Modules:
  0.0 73.1 jit_solution(14452212466683131063)
XLA Ops:
  1.3 69.9 %shard_map.95 = (f32[8,343]{1,0:T(8,128)}, f32[8,343]{1,0:T(8,128)}) custom-call(f32[8]{0:T(128)} %cond_ref.1, s32[1]{0:T(128)S(6)} %copy.12.count_ref, f32[8,343]{1,0:T(8,128)} %src_ref.1, f32[64,8,343]{2,1,0:T(8,128)} %basis_ref.1, bf16[343,256]{1,0:T(8,128)(2,1)} %bitcast.3, s32[1,256]{1,0:T(1,128)} %bitcast.4, s32[1,256]{1,0:T(1,128)} %bitcast.5, ...), custom_call_target="tpu_custom_call" | custom-call | tf_op jit(solution)/shard_map/pallas_call | solution.py:460
  71.2 0.0 copy-start
  71.2 1.3 %copy.13 = f32[8,343]{1,0:T(8,128)} copy(f32[8,343]{1,0:T(8,128)} %get-tuple-element.4) | data formatting | bytes 21952
  72.5 0.0 copy-done
  72.5 0.6 copy.14
Async XLA Ops:
  71.2 1.3 %copy-start = (f32[8,343]{1,0:T(8,128)S(1)}, f32[8,343]{1,0:T(8,128)}, u32[]{:S(2)}) copy-start(f32[8,343]{1,0:T(8,128)} %get-tuple-element.5) | copy-start | bytes 32932

commit v3 on v2

--- a/solution.py
+++ b/solution.py
@@ -17,6 +17,7 @@
 NB = 64
 XN = 4
 MARK = 120
+EARLY = 24
 SHIFT = 1.0
 PENALTY = 10.0
 RELAX = 0.2
@@ -68,8 +69,7 @@
     elem_ref,
     own_ref,
     kel_ref,
-    x_out,
-    r_out,
+    out_ref,
     cond_in,
     count_in,
     src_in,
@@ -98,6 +98,7 @@
     f_sem,
     s_sem,
     in_sem,
+    relay_sem,
 ):
     zn = subs // XN
     total = slabs * subs
@@ -129,8 +130,9 @@
         other = lax.rem(chain + step + total, total)
         return (lax.div(other, subs), lax.rem(other, subs))
 
+    reach = min(4, zn // 2)
     peers = (
-        [z_peer(i) for i in far]
+        [z_peer(i) for i in far if min(i, zn - i) <= reach]
         + [chain_peer(step) for step in (-2, 2, -1, 1)]
         + [plane_peer(i, j) for i, j in plane]
         + [core_peer]
@@ -194,6 +196,11 @@
     a_src[:, :, 256:NODES] = moved[:, 256:].reshape(XN, slot, NODES - 256)
 
     pl.semaphore_wait(barrier, len(peers))
+    relays = [z_peer(reach), z_peer(zn - reach)] if zn // 2 > reach else []
+    for peer in relays:
+        pl.semaphore_signal(
+            relay_sem, inc=1, device_id=peer, device_id_type=pl.DeviceIdType.MESH
+        )
     a_copies = [
         send(a_src.at[lax.rem(x + i, XN)], a_dst.at[i], a_sem, i, x_peer(i))
         for i in x_order
@@ -235,6 +242,17 @@
         applied.append(out)
     matrix = dot(bt_ref[...], jnp.concatenate(applied, axis=1), NT, HIGH)
 
+    unit = (iota((NB, NB), 0) == iota((NB, NB), 1)).astype(F32)
+    work = jnp.concatenate([matrix, unit], axis=1)
+    row_id = iota((NB, 2 * NB), 0)
+
+    def eliminate(work, k):
+        row = work[k : k + 1, :] / work[k : k + 1, k : k + 1]
+        return jnp.where(row_id == k, row, work - work[:, k : k + 1] * row)
+
+    for k in range(EARLY):
+        work = eliminate(work, k)
+
     for copy in a_copies:
         copy.wait()
     arrived = a_dst[...].reshape(XN * slot, WIDE)
@@ -243,6 +261,8 @@
     keep = lax.rem(iota(spread.shape, 0), zn) == lax.div(iota(spread.shape, 1), EL)
     weights = jnp.where(keep, spread, 0.0)
     sums = dot(weights.T.astype(BF16), arrived)
+    if relays:
+        pl.semaphore_wait(relay_sem, len(relays))
     b_src[...] = sums[: zn * EL].reshape(zn, EL, WIDE)
     b_copies = [
         send(b_src.at[lax.rem(z + i, zn)], b_dst.at[i], b_sem, i, z_peer(i))
@@ -250,12 +270,8 @@
     ]
     b_dst[0] = b_src[z]
 
-    unit = (iota((NB, NB), 0) == iota((NB, NB), 1)).astype(F32)
-    work = jnp.concatenate([matrix, unit], axis=1)
-    row_id = iota((NB, 2 * NB), 0)
-    for k in range(NB):
-        row = work[k : k + 1, :] / work[k : k + 1, k : k + 1]
-        work = jnp.where(row_id == k, row, work - work[:, k : k + 1] * row)
+    for k in range(EARLY, NB):
+        work = eliminate(work, k)
     inverse = work[:, NB:]
     cz_ref[...] = dot(inverse, bt_ref[...], precision=HIGH)
 
@@ -443,8 +459,8 @@
             inner = fresh
     answer = sum(sol_c[j] * preconds[j] for j in range(3))
     remain = sum(res_c[j] * residuals[j] for j in range(4))
-    x_out[...] = answer[:, :NODES]
-    r_out[...] = remain[:, :NODES]
+    out_ref[0] = answer
+    out_ref[1] = remain
 
 
 def on_device(slabs, subs, source, conductivity, basis, values, elements, owners, counts):
@@ -456,12 +472,12 @@
     slot = zn * CAP
     peers = XN * (slabs // 2) - 1 + 1 + zn - 1
     dma = pltpu.SemaphoreType.DMA
-    out = jax.ShapeDtypeStruct(source.shape, F32)
-    return pl.pallas_call(
+    out = jax.ShapeDtypeStruct((2, EL, WIDE), F32)
+    both = pl.pallas_call(
         functools.partial(kernel, slabs, subs),
-        out_shape=(out, out),
+        out_shape=out,
         in_specs=[hbm] * 8,
-        out_specs=(vmem, vmem),
+        out_specs=vmem,
         scratch_shapes=[
             pltpu.SMEM((EL,), F32),
             pltpu.SMEM((1,), jnp.int32),
@@ -491,6 +507,7 @@
             dma((2, 12)),
             dma((2, peers)),
             dma((8,)),
+            pltpu.SemaphoreType.REGULAR,
         ],
         compiler_params=pltpu.CompilerParams(
             collective_id=0, has_side_effects=True, vmem_limit_bytes=60 * 1024 * 1024
@@ -505,6 +522,7 @@
         owners.reshape(1, rows),
         jnp.asarray(kel, BF16),
     )
+    return both[0, :, :NODES], both[1, :, :NODES]
 
 
 def solution(mesh):

time: 73.3 us -> 68.1 us (0.929)
  Pallas kernels: 69.9 us -> 65.3 us
    pallas_call x1, Pallas kernels: 69.9 us -> 65.3 us  [on_device(): pl.pallas_call(functools.partial(kernel, slabs, subs), out_shape=out, in_...]
    unnamed x4 -> x0, local copies, waits for them, and re-layouts: 1.92 us -> none
    squeeze x0 -> x1, local copies, waits for them, and re-layouts: none -> 1.33 us  [on_device(): return (both[0, :, :NODES], both[1, :, :NODES])]
where the time goes in v3:
time: 68.1 us; the launch traced here: 67.9 us
  Pallas kernels  65.3 us (96%)
  local copies, waits for them, and re-layouts  1.33 us (2%)
  between operations  1.29 us (2%)
    pallas_call x1, Pallas kernels, on_device(): pl.pallas_call(functools.partial(kernel, slabs, subs), out_shape=out, in_...  65.3 us

profile of v3, /device:TPU:1, one launch (start us, length us, event | category | flops | bytes accessed | tf_op | source)
XLA Modules:
  0.0 67.9 jit_solution(3986113058051032338)
XLA Ops:
  1.3 65.3 %shard_map.95 = f32[2,8,384]{2,1,0:T(8,128)} custom-call(f32[8]{0:T(128)} %cond_ref.1, s32[1]{0:T(128)S(6)} %copy.10.count_ref, f32[8,343]{1,0:T(8,128)} %src_ref.1, f32[64,8,343]{2,1,0:T(8,128)} %basis_ref.1, bf16[343,256]{1,0:T(8,128)(2,1)} %bitcast.7, s32[1,256]{1,0:T(1,128)} %bitcast.8, s32[1,256]{1,0:T(1,128)} %bitcast.9, ...), custom_call_target="tpu_custom_call" | custom-call | tf_op jit(solution)/shard_map/pallas_call | solution.py:476
  66.5 1.3 %slice_bitcast_fusion = (f32[8,343]{1,0:T(8,128)}, f32[8,343]{1,0:T(8,128)}) fusion(f32[2,8,384]{2,1,0:T(8,128)} %shard_map.95), kind=kLoop, calls=%fused_computation | loop fusion | bytes 43904 | tf_op jit(solution)/shard_map/squeeze | solution.py:525

commit v4 on v3

--- a/solution.py
+++ b/solution.py
@@ -133,9 +133,8 @@
     reach = min(4, zn // 2)
     peers = (
         [z_peer(i) for i in far if min(i, zn - i) <= reach]
-        + [chain_peer(step) for step in (-2, 2, -1, 1)]
-        + [plane_peer(i, j) for i, j in plane]
-        + [core_peer]
+        + [(lax.rem(slab + i, slabs), sub) for i in range(1, slabs)]
+        + [x_peer(i) for i in x_order]
     )
     barrier = pltpu.get_barrier_semaphore()
     for peer in peers:
@@ -172,6 +171,12 @@
     ]
     for fetch in fetches:
         fetch.start()
+
+    leaving = []
+
+    def settle():
+        while leaving:
+            leaving.pop(0).wait_send()
 
     for fetch in fetches[:4]:
         fetch.wait()
@@ -254,7 +259,7 @@
         work = eliminate(work, k)
 
     for copy in a_copies:
-        copy.wait()
+        copy.wait_recv()
     arrived = a_dst[...].reshape(XN * slot, WIDE)
     spread = (iota((128, 128), 0) == MARK + lax.rem(iota((128, 128), 1), EL)).astype(BF16)
     spread = dot(arrived[:, 256:], spread)
@@ -269,6 +274,8 @@
         for i in far
     ]
     b_dst[0] = b_src[z]
+    leaving.extend(a_copies)
+    settle()
 
     for k in range(EARLY, NB):
         work = eliminate(work, k)
@@ -292,11 +299,6 @@
     face_r = right_face(element(bt_ref, EL - 1))
     g_src[0] = dot(face_l.T, w, precision=HIGH)[:56]
     g_src[1] = dot(face_r.T, w, precision=HIGH)[:56]
-    g_copies = [
-        send(g_src.at[0], g_dst.at[0], g_sem, 0, chain_peer(-1)),
-        send(g_src.at[1], g_dst.at[1], g_sem, 1, chain_peer(1)),
-    ]
-
     el_row = iota((EL, WIDE), 0)
     conduct = jnp.zeros((EL, WIDE), F32)
     for e in range(EL):
@@ -307,7 +309,12 @@
     source_ref[:, 256:] = jnp.zeros((EL, 128), F32)
     source_ref[:, :NODES] = src_in[...]
     for copy in b_copies:
-        copy.wait()
+        copy.wait_recv()
+    g_copies = [
+        send(g_src.at[0], g_dst.at[0], g_sem, 0, chain_peer(-1)),
+        send(g_src.at[1], g_dst.at[1], g_sem, 1, chain_peer(1)),
+    ]
+    leaving.extend(b_copies + g_copies)
     currents = b_dst[0]
     for i in range(1, zn):
         currents = currents + b_dst[i]
@@ -352,30 +359,31 @@
             send(f_src.at[k], f_dst.at[k, i], f_sem, 4 * k + i, chain_peer(step))
             for i, step in ((2, -2), (3, 2), (0, -1), (1, 1))
         ]
+        settle()
+        leaving.extend(copies)
         for i in range(k + 1):
             for j in range(k):
                 if (i, j) not in products:
                     products[i, j] = gram(residuals[i], preconds[j])
         partial = scaled + first
-        if k == 0:
-            for copy in g_copies:
-                copy.wait()
-        for copy in copies:
-            copy.wait()
+        for copy in copies[2:]:
+            copy.wait_recv()
         after1 = jnp.where(has[1], f_dst[k, 0], 0.0)
         before1 = jnp.where(has[-1], f_dst[k, 1], 0.0)
-        after2 = jnp.where(has[2], f_dst[k, 2], 0.0)
-        before2 = jnp.where(has[-2], f_dst[k, 3], 0.0)
         own_v = before1[1:2] + pltpu.roll(after1[0:1], 64, 1)
-        after_v = fr + pltpu.roll(after2[0:1], 64, 1)
-        before_v = before2[1:2] + pltpu.roll(fl, 64, 1)
         pre = partial + lift(jnp.sum(w * own_v, axis=1, keepdims=True))
-        after_face = jnp.where(has[1], after1[2:3] + turn(g_dst[0], after_v), 0.0)
-        before_face = jnp.where(has[-1], before1[3:4] + turn(g_dst[1], before_v), 0.0)
         hi, lo = split2(pre)
         both = jnp.concatenate([hi.astype(F32), lo.astype(F32)], axis=0).astype(BF16)
         stiff = dot(both, kel)
         stiff = stiff[0:EL] + stiff[EL : 2 * EL]
+        for copy in copies[:2] + (g_copies if k == 0 else []):
+            copy.wait_recv()
+        after2 = jnp.where(has[2], f_dst[k, 2], 0.0)
+        before2 = jnp.where(has[-2], f_dst[k, 3], 0.0)
+        after_v = fr + pltpu.roll(after2[0:1], 64, 1)
+        before_v = before2[1:2] + pltpu.roll(fl, 64, 1)
+        after_face = jnp.where(has[1], after1[2:3] + turn(g_dst[0], after_v), 0.0)
+        before_face = jnp.where(has[-1], before1[3:4] + turn(g_dst[1], before_v), 0.0)
         from_left = pltpu.roll(pltpu.roll(pre, 1, 0), WIDE - NODES + FACE, 1)
         from_left = jnp.where(
             el_row == 0, jnp.concatenate([before_face, pad_row], axis=1), from_left
@@ -415,8 +423,10 @@
             send(s_src.at[stage], s_dst.at[at + i], s_sem, at + i, peer)
             for i, peer in enumerate(to)
         ]
+        settle()
+        leaving.extend(copies)
         for copy in copies:
-            copy.wait()
+            copy.wait_recv()
         for i in range(len(to)):
             share = share + s_dst[at + i]
         at += len(to)
@@ -459,6 +469,7 @@
             inner = fresh
     answer = sum(sol_c[j] * preconds[j] for j in range(3))
     remain = sum(res_c[j] * residuals[j] for j in range(4))
+    settle()
     out_ref[0] = answer
     out_ref[1] = remain
 

time: 68.1 us -> 63.7 us (0.935)
  Pallas kernels: 65.3 us -> 60.9 us
    pallas_call x1, Pallas kernels: 65.3 us -> 60.9 us  [on_device(): pl.pallas_call(functools.partial(kernel, slabs, subs), out_shape=out, in_...]
where the time goes in v4:
time: 63.7 us; the launch traced here: 63.5 us
  Pallas kernels  60.9 us (96%)
  local copies, waits for them, and re-layouts  1.33 us (2%)
  between operations  1.29 us (2%)
    pallas_call x1, Pallas kernels, on_device(): pl.pallas_call(functools.partial(kernel, slabs, subs), out_shape=out, in_...  60.9 us
    squeeze x1, local copies, waits for them, and re-layouts, on_device(): return (both[0, :, :NODES], both[1, :, :NODES])  1.33 us

profile of v4, /device:TPU:1, one launch (start us, length us, event | category | flops | bytes accessed | tf_op | source)
XLA Modules:
  0.0 63.5 jit_solution(16266140338254734009)
XLA Ops:
  1.3 60.9 %shard_map.95 = f32[2,8,384]{2,1,0:T(8,128)} custom-call(f32[8]{0:T(128)} %cond_ref.1, s32[1]{0:T(128)S(6)} %copy.10.count_ref, f32[8,343]{1,0:T(8,128)} %src_ref.1, f32[64,8,343]{2,1,0:T(8,128)} %basis_ref.1, bf16[343,256]{1,0:T(8,128)(2,1)} %bitcast.7, s32[1,256]{1,0:T(1,128)} %bitcast.8, s32[1,256]{1,0:T(1,128)} %bitcast.9, ...), custom_call_target="tpu_custom_call" | custom-call | tf_op jit(solution)/shard_map/pallas_call | solution.py:487
  62.1 1.3 %slice_bitcast_fusion = (f32[8,343]{1,0:T(8,128)}, f32[8,343]{1,0:T(8,128)}) fusion(f32[2,8,384]{2,1,0:T(8,128)} %shard_map.95), kind=kLoop, calls=%fused_computation | loop fusion | bytes 43904 | tf_op jit(solution)/shard_map/squeeze | solution.py:536

commit v5 on v4

--- a/solution.py
+++ b/solution.py
@@ -130,7 +130,7 @@
         other = lax.rem(chain + step + total, total)
         return (lax.div(other, subs), lax.rem(other, subs))
 
-    reach = min(4, zn // 2)
+    reach = min(3, zn // 2)
     peers = (
         [z_peer(i) for i in far if min(i, zn - i) <= reach]
         + [(lax.rem(slab + i, slabs), sub) for i in range(1, slabs)]
@@ -201,15 +201,25 @@
     a_src[:, :, 256:NODES] = moved[:, 256:].reshape(XN, slot, NODES - 256)
 
     pl.semaphore_wait(barrier, len(peers))
-    relays = [z_peer(reach), z_peer(zn - reach)] if zn // 2 > reach else []
-    for peer in relays:
-        pl.semaphore_signal(
-            relay_sem, inc=1, device_id=peer, device_id_type=pl.DeviceIdType.MESH
-        )
+    hops = [h for h in (min(reach, zn // 2 - reach), zn // 2 - 2 * reach) if h > 0]
+
+    def vouch(k):
+        if k > 0 and k <= len(hops):
+            pl.semaphore_wait(relay_sem.at[k - 1], 2)
+        if k < len(hops):
+            for peer in (z_peer(hops[k]), z_peer(zn - hops[k])):
+                pl.semaphore_signal(
+                    relay_sem.at[k],
+                    inc=1,
+                    device_id=peer,
+                    device_id_type=pl.DeviceIdType.MESH,
+                )
+
     a_copies = [
         send(a_src.at[lax.rem(x + i, XN)], a_dst.at[i], a_sem, i, x_peer(i))
         for i in x_order
     ]
+    vouch(0)
     a_dst[0] = a_src[x]
 
     for fetch in fetches[4:]:
@@ -255,19 +265,19 @@
         row = work[k : k + 1, :] / work[k : k + 1, k : k + 1]
         return jnp.where(row_id == k, row, work - work[:, k : k + 1] * row)
 
+    vouch(1)
     for k in range(EARLY):
         work = eliminate(work, k)
 
     for copy in a_copies:
         copy.wait_recv()
     arrived = a_dst[...].reshape(XN * slot, WIDE)
-    spread = (iota((128, 128), 0) == MARK + lax.rem(iota((128, 128), 1), EL)).astype(BF16)
-    spread = dot(arrived[:, 256:], spread)
-    keep = lax.rem(iota(spread.shape, 0), zn) == lax.div(iota(spread.shape, 1), EL)
-    weights = jnp.where(keep, spread, 0.0)
-    sums = dot(weights.T.astype(BF16), arrived)
-    if relays:
-        pl.semaphore_wait(relay_sem, len(relays))
+    pick = (iota((128, 128), 1) == MARK + lax.rem(iota((128, 128), 0), EL)).astype(BF16)
+    spread = dot(pick, arrived[:, 256:], NT)
+    keep = lax.rem(iota(spread.shape, 1), zn) == lax.div(iota(spread.shape, 0), EL)
+    weights = jnp.where(keep, spread, 0.0).astype(BF16)
+    sums = dot(weights, arrived)
+    vouch(2)
     b_src[...] = sums[: zn * EL].reshape(zn, EL, WIDE)
     b_copies = [
         send(b_src.at[lax.rem(z + i, zn)], b_dst.at[i], b_sem, i, z_peer(i))
@@ -310,11 +320,7 @@
     source_ref[:, :NODES] = src_in[...]
     for copy in b_copies:
         copy.wait_recv()
-    g_copies = [
-        send(g_src.at[0], g_dst.at[0], g_sem, 0, chain_peer(-1)),
-        send(g_src.at[1], g_dst.at[1], g_sem, 1, chain_peer(1)),
-    ]
-    leaving.extend(b_copies + g_copies)
+    leaving.extend(b_copies)
     currents = b_dst[0]
     for i in range(1, zn):
         currents = currents + b_dst[i]
@@ -349,9 +355,9 @@
         for e in range(EL):
             acc = acc + element(cz_ref, e) * res[e : e + 1, :]
         acc = acc[:, 0:128] + acc[:, 128:256] + acc[:, 256:384]
-        first = lift(jnp.sum(acc, axis=1, keepdims=True))
-        fl = left_face(first[0:1])
-        fr = right_face(first[EL - 1 : EL])
+        coarse = jnp.sum(acc, axis=1, keepdims=True)
+        fl = jnp.sum(face_l * coarse, axis=0, keepdims=True)
+        fr = jnp.sum(face_r * coarse, axis=0, keepdims=True)
         el = left_face(scaled[0:1]) + fl
         er = right_face(scaled[EL - 1 : EL]) + fr
         f_src[k] = jnp.concatenate([fl, fr, el, er, jnp.zeros((4, 128), F32)], axis=0)
@@ -359,13 +365,19 @@
             send(f_src.at[k], f_dst.at[k, i], f_sem, 4 * k + i, chain_peer(step))
             for i, step in ((2, -2), (3, 2), (0, -1), (1, 1))
         ]
+        if k == 0:
+            g_copies = [
+                send(g_src.at[0], g_dst.at[0], g_sem, 0, chain_peer(-1)),
+                send(g_src.at[1], g_dst.at[1], g_sem, 1, chain_peer(1)),
+            ]
+            leaving.extend(g_copies)
         settle()
         leaving.extend(copies)
         for i in range(k + 1):
             for j in range(k):
                 if (i, j) not in products:
                     products[i, j] = gram(residuals[i], preconds[j])
-        partial = scaled + first
+        partial = scaled + lift(coarse)
         for copy in copies[2:]:
             copy.wait_recv()
         after1 = jnp.where(has[1], f_dst[k, 0], 0.0)
@@ -518,7 +530,7 @@
             dma((2, 12)),
             dma((2, peers)),
             dma((8,)),
-            pltpu.SemaphoreType.REGULAR,
+            pltpu.SemaphoreType.REGULAR((2,)),
         ],
         compiler_params=pltpu.CompilerParams(
             collective_id=0, has_side_effects=True, vmem_limit_bytes=60 * 1024 * 1024

time: 63.7 us -> 62 us (0.973)
  Pallas kernels: 60.9 us -> 59.2 us
    pallas_call x1, Pallas kernels: 60.9 us -> 59.2 us  [on_device(): pl.pallas_call(functools.partial(kernel, slabs, subs), out_shape=out, in_...]
where the time goes in v5:
time: 62 us; the launch traced here: 61.8 us
  Pallas kernels  59.2 us (95%)
  local copies, waits for them, and re-layouts  1.33 us (2%)
  between operations  1.29 us (2%)
    pallas_call x1, Pallas kernels, on_device(): pl.pallas_call(functools.partial(kernel, slabs, subs), out_shape=out, in_...  59.2 us
    squeeze x1, local copies, waits for them, and re-layouts, on_device(): return (both[0, :, :NODES], both[1, :, :NODES])  1.33 us

profile of v5, /device:TPU:1, one launch (start us, length us, event | category | flops | bytes accessed | tf_op | source)
XLA Modules:
  0.0 61.8 jit_solution(350406612282791803)
XLA Ops:
  1.3 59.2 %shard_map.95 = f32[2,8,384]{2,1,0:T(8,128)} custom-call(f32[8]{0:T(128)} %cond_ref.1, s32[1]{0:T(128)S(6)} %copy.10.count_ref, f32[8,343]{1,0:T(8,128)} %src_ref.1, f32[64,8,343]{2,1,0:T(8,128)} %basis_ref.1, bf16[343,256]{1,0:T(8,128)(2,1)} %bitcast.7, s32[1,256]{1,0:T(1,128)} %bitcast.8, s32[1,256]{1,0:T(1,128)} %bitcast.9, ...), custom_call_target="tpu_custom_call" | custom-call | tf_op jit(solution)/shard_map/pallas_call | solution.py:499
  60.5 1.3 %slice_bitcast_fusion = (f32[8,343]{1,0:T(8,128)}, f32[8,343]{1,0:T(8,128)}) fusion(f32[2,8,384]{2,1,0:T(8,128)} %shard_map.95), kind=kLoop, calls=%fused_computation | loop fusion | bytes 43904 | tf_op jit(solution)/shard_map/squeeze | solution.py:548

commit v6 on v5

--- a/solution.py
+++ b/solution.py
@@ -215,9 +215,19 @@
                     device_id_type=pl.DeviceIdType.MESH,
                 )
 
-    a_copies = [
-        send(a_src.at[lax.rem(x + i, XN)], a_dst.at[i], a_sem, i, x_peer(i))
-        for i in x_order
+    parts = (slice(256, WIDE), slice(0, 256))
+    a_parts = [
+        [
+            send(
+                a_src.at[lax.rem(x + i, XN), :, part],
+                a_dst.at[i, :, part],
+                a_sem,
+                p * XN + i,
+                x_peer(i),
+            )
+            for i in x_order
+        ]
+        for p, part in enumerate(parts)
     ]
     vouch(0)
     a_dst[0] = a_src[x]
@@ -269,20 +279,34 @@
     for k in range(EARLY):
         work = eliminate(work, k)
 
-    for copy in a_copies:
-        copy.wait_recv()
-    arrived = a_dst[...].reshape(XN * slot, WIDE)
-    pick = (iota((128, 128), 1) == MARK + lax.rem(iota((128, 128), 0), EL)).astype(BF16)
-    spread = dot(pick, arrived[:, 256:], NT)
-    keep = lax.rem(iota(spread.shape, 1), zn) == lax.div(iota(spread.shape, 0), EL)
-    weights = jnp.where(keep, spread, 0.0).astype(BF16)
-    sums = dot(weights, arrived)
-    vouch(2)
-    b_src[...] = sums[: zn * EL].reshape(zn, EL, WIDE)
-    b_copies = [
-        send(b_src.at[lax.rem(z + i, zn)], b_dst.at[i], b_sem, i, z_peer(i))
-        for i in far
-    ]
+    b_parts = []
+    for p, part in enumerate(parts):
+        for copy in a_parts[p]:
+            copy.wait_recv()
+        arrived = a_dst[:, :, part].reshape(XN * slot, part.stop - part.start)
+        if p == 0:
+            pick = iota((128, 128), 1) == MARK + lax.rem(iota((128, 128), 0), EL)
+            spread = dot(pick.astype(BF16), arrived, NT)
+            keep = lax.rem(iota(spread.shape, 1), zn) == lax.div(iota(spread.shape, 0), EL)
+            weights = jnp.where(keep, spread, 0.0).astype(BF16)
+        sums = dot(weights, arrived)[: zn * EL]
+        b_src[:, :, part] = sums.reshape(zn, EL, part.stop - part.start)
+        if p == 0:
+            vouch(2)
+        b_parts.append(
+            [
+                send(
+                    b_src.at[lax.rem(z + i, zn), :, part],
+                    b_dst.at[i, :, part],
+                    b_sem,
+                    p * zn + i,
+                    z_peer(i),
+                )
+                for i in far
+            ]
+        )
+    a_copies = a_parts[0] + a_parts[1]
+    b_copies = b_parts[0] + b_parts[1]
     b_dst[0] = b_src[z]
     leaving.extend(a_copies)
     settle()
@@ -524,8 +548,8 @@
             pltpu.VMEM((3, 4, 8, 128), F32),
             pltpu.VMEM((3, 8, 128), F32),
             pltpu.VMEM((peers, 8, 128), F32),
-            dma((2, XN)),
-            dma((2, zn)),
+            dma((2, 2 * XN)),
+            dma((2, 2 * zn)),
             dma((2, 2)),
             dma((2, 12)),
             dma((2, peers)),

time: 62 us -> 62.1 us (level)
  no operation moved by 1% of the time
where the time goes in v6:
time: 62.1 us; the launch traced here: 61.8 us
  Pallas kernels  59.2 us (95%)
  local copies, waits for them, and re-layouts  1.33 us (2%)
  between operations  1.29 us (2%)
    pallas_call x1, Pallas kernels, on_device(): pl.pallas_call(functools.partial(kernel, slabs, subs), out_shape=out, in_...  59.2 us
    squeeze x1, local copies, waits for them, and re-layouts, on_device(): return (both[0, :, :NODES], both[1, :, :NODES])  1.33 us

profile of v6, /device:TPU:1, one launch (start us, length us, event | category | flops | bytes accessed | tf_op | source)
XLA Modules:
  0.0 61.8 jit_solution(15990625619568507729)
XLA Ops:
  1.3 59.2 %shard_map.95 = f32[2,8,384]{2,1,0:T(8,128)} custom-call(f32[8]{0:T(128)} %cond_ref.1, s32[1]{0:T(128)S(6)} %copy.10.count_ref, f32[8,343]{1,0:T(8,128)} %src_ref.1, f32[64,8,343]{2,1,0:T(8,128)} %basis_ref.1, bf16[343,256]{1,0:T(8,128)(2,1)} %bitcast.7, s32[1,256]{1,0:T(1,128)} %bitcast.8, s32[1,256]{1,0:T(1,128)} %bitcast.9, ...), custom_call_target="tpu_custom_call" | custom-call | tf_op jit(solution)/shard_map/pallas_call | solution.py:523
  60.4 1.3 %slice_bitcast_fusion = (f32[8,343]{1,0:T(8,128)}, f32[8,343]{1,0:T(8,128)}) fusion(f32[2,8,384]{2,1,0:T(8,128)} %shard_map.95), kind=kLoop, calls=%fused_computation | loop fusion | bytes 43904 | tf_op jit(solution)/shard_map/squeeze | solution.py:572

commit v7 on v5

--- a/solution.py
+++ b/solution.py
@@ -17,7 +17,7 @@
 NB = 64
 XN = 4
 MARK = 120
-EARLY = 24
+EARLY = 8
 SHIFT = 1.0
 PENALTY = 10.0
 RELAX = 0.2

time: 62 us -> 62 us (level)
  no operation moved by 1% of the time
where the time goes in v7:
time: 62 us; the launch traced here: 61.8 us
  Pallas kernels  59.2 us (95%)
  local copies, waits for them, and re-layouts  1.33 us (2%)
  between operations  1.29 us (2%)
    pallas_call x1, Pallas kernels, on_device(): pl.pallas_call(functools.partial(kernel, slabs, subs), out_shape=out, in_...  59.2 us
    squeeze x1, local copies, waits for them, and re-layouts, on_device(): return (both[0, :, :NODES], both[1, :, :NODES])  1.33 us

profile of v7, /device:TPU:1, one launch (start us, length us, event | category | flops | bytes accessed | tf_op | source)
XLA Modules:
  0.0 61.8 jit_solution(691119457249862351)
XLA Ops:
  1.3 59.2 %shard_map.95 = f32[2,8,384]{2,1,0:T(8,128)} custom-call(f32[8]{0:T(128)} %cond_ref.1, s32[1]{0:T(128)S(6)} %copy.10.count_ref, f32[8,343]{1,0:T(8,128)} %src_ref.1, f32[64,8,343]{2,1,0:T(8,128)} %basis_ref.1, bf16[343,256]{1,0:T(8,128)(2,1)} %bitcast.7, s32[1,256]{1,0:T(1,128)} %bitcast.8, s32[1,256]{1,0:T(1,128)} %bitcast.9, ...), custom_call_target="tpu_custom_call" | custom-call | tf_op jit(solution)/shard_map/pallas_call | solution.py:499
  60.5 1.3 %slice_bitcast_fusion = (f32[8,343]{1,0:T(8,128)}, f32[8,343]{1,0:T(8,128)}) fusion(f32[2,8,384]{2,1,0:T(8,128)} %shard_map.95), kind=kLoop, calls=%fused_computation | loop fusion | bytes 43904 | tf_op jit(solution)/shard_map/squeeze | solution.py:548
